TPU v7x, 128 devices: a whole 4x4x4 slice. The times are simulated.
128 devices in a mesh: wave: 32 (over x, z, core), lat: 4 (over y).
Axes of the slice: x: 4, y: 4, z: 4, core: 2. Of those that a mesh axis runs over, the one named last changes fastest.
Arguments:
- spectra: bfloat16 [1280, 1280, 128], P('wave', 'lat'), may hold values from -0.1796875 to 0.1796875
- legendre: bfloat16 [1280, 1280, 128], P('wave', 'lat'), may hold values from -0.25 to 0.25
- wave_list: int32 [1280], replicated, may hold values from 0 to 1279, as said below
- cycle_lons: int32 [128], replicated, may hold values from 20 to 5136, as said below
Outputs:
- grid_out: bfloat16 [128, 5632, 64], P('lat', 'wave')
Inputs may be any that keep to these rules, and one draw needn't show every extreme that they name: `wave_list`: A permutation of the wavenumbers; the 1280 // 32 slots of each index of wave hold whole pairs m and 1279 - m. `cycle_lons`: window rows run from north to south, one row from each run of 20 Gaussian latitudes; a row on latitude cycle i counted from the nearer pole has 20 + 4 i longitudes. The first row is on cycle 0 and some row is on the equator's cycle.
All inputs are finite; a program needn't handle non-finite values.
Results may differ from a plain program's by a relative error of at most 0.015.
Values may be sent and summed in bfloat16 or wider, within the bound.
A program may use at most 64 MiB of HBM per device.

v0:
```python
import math

import jax
import jax.numpy as jnp
from jax import lax
from jax.sharding import PartitionSpec as P

M = 1280
F = 64
NLONP = 5632


TWO_PI = 2.0 * math.pi
BLOCK = 512


def lon_block_table(wave_numbers, row_lons, k_first, k_count):
    k_index = k_first + jnp.arange(k_count, dtype=jnp.int32)
    turn_index = k_index[:, None] * wave_numbers[None, :] % row_lons
    angles = turn_index.astype(jnp.float32) * (TWO_PI / row_lons.astype(jnp.float32))
    weights = jnp.where(
        wave_numbers == 0, 1.0, jnp.where(2 * wave_numbers < row_lons, 2.0, 0.0)
    ).astype(jnp.float32)
    scales = jnp.where((k_index < row_lons)[:, None], weights[None, :], 0.0)
    cosine_part = (scales * jnp.cos(angles)).astype(jnp.bfloat16)
    sine_part = (scales * -jnp.sin(angles)).astype(jnp.bfloat16)
    return jnp.concatenate([cosine_part, sine_part], 1)


def local(spectra, legendre, wave_list, cycle_lons):
    slot_count = spectra.shape[0]
    row_depth = spectra.shape[1]
    band_rows = legendre.shape[2] // lax.axis_size("lat")
    wave_count = lax.axis_size("wave")
    rows_each = band_rows // wave_count
    wave_at = lax.axis_index("wave")
    lat_at = lax.axis_index("lat")
    my_waves = lax.dynamic_slice_in_dim(wave_list, wave_at * slot_count, slot_count)
    offsets = lat_at * row_depth + jnp.arange(row_depth, dtype=jnp.int32)
    live_mask = (offsets[None, :] < (M - my_waves)[:, None])[:, :, None]
    masked = jnp.where(live_mask, spectra, jnp.zeros_like(spectra))
    fourier = lax.psum_scatter(
        jnp.einsum("sjw,sjc->wsc", legendre, masked, preferred_element_type=jnp.float32).astype(
            jnp.bfloat16
        ),
        "lat",
        scatter_dimension=0,
        tiled=True,
    )
    band_lons = lax.dynamic_slice_in_dim(cycle_lons, lat_at * band_rows, band_rows)
    moved_rows = lax.all_to_all(fourier, "wave", split_axis=0, concat_axis=1, tiled=True)
    my_lons = lax.dynamic_slice_in_dim(band_lons, wave_at * rows_each, rows_each)
    slot_total = NLONP

    def one_row(args):
        fourier_row, row_lons = args
        stacked = jnp.concatenate([fourier_row[:, :F], fourier_row[:, F:]], 0)

        def compute_block(k_first):
            table = lon_block_table(wave_list, row_lons, k_first, BLOCK)
            return jnp.dot(table, stacked, preferred_element_type=jnp.float32)

        def lon_block(k_first):
            return compute_block(k_first)

        starts = jnp.arange(slot_total // BLOCK, dtype=jnp.int32) * BLOCK
        return lax.map(lon_block, starts).reshape(slot_total, F).astype(jnp.bfloat16)

    rows_grid = lax.map(one_row, (moved_rows, my_lons))
    lon_columns = lax.all_to_all(rows_grid, "wave", split_axis=1, concat_axis=0, tiled=True)
    return lon_columns


def solution(mesh):
    in_specs = (P("wave", "lat", None), P("wave", "lat", None), P(), P())
    out_specs = P("lat", "wave", None)
    return jax.shard_map(local, mesh=mesh, in_specs=in_specs, out_specs=out_specs, check_vma=False)
```

profile of v0, /device:TPU:1, one launch (start us, length us, event | category | flops | bytes accessed | tf_op | source)
XLA Modules:
  0.0 597.0 jit_solution(1265195110858603028)
XLA Ops:
  8.5 6.5 %fusion.26 = bf16[128,40,128]{0,2,1:T(8,128)(2,1)} fusion(bf16[40,320,128]{2,1,0:T(8,128)(2,1)S(1)} %copy-done, bf16[40,320,128]{2,1,0:T(8,128)(2,1)} %param.6, pred[40,320]{1,0:T(8,128)(4,1)S(1)} %broadcast_compare_fusion.1), kind=kOutput, calls=%fused_computation.28 | convolution fusion | flops 421724160 | bytes 7877120 | tf_op jit(solution)/shard_map/sjw,sjc->wsc/dot_general | solution.py:43
  15.0 2.7 copy.8
  17.8 26.6 %reduce-scatter.2.cloned.1.call-done = bf16[32,40,128]{2,1,0:T(8,128)(2,1)} async-done(((bf16[128,40,128]{2,1,0:T(8,128)(2,1)}), bf16[32,40,128]{2,1,0:T(8,128)(2,1)}) %reduce-scatter.2.cloned.1.call-update) | async-done | bytes 327696 | tf_op jit(solution)/shard_map/reduce_scatter | solution.py:42
  44.4 9.0 %all-to-all-start = ((bf16[32,40,128]{2,1,0:T(8,128)(2,1)}), bf16[32,40,128]{2,1,0:T(8,128)(2,1)}, u32[]{:S(2)}, u32[]{:S(2)}) async-start(bf16[32,40,128]{2,1,0:T(8,128)(2,1)} %reduce-scatter.2.cloned.1.call-done), calls=%async_computation.1 | async-start | bytes 655360 | tf_op jit(solution)/shard_map/all_to_all | solution.py:51
  55.7 7.4 %all-to-all-done = bf16[32,40,128]{2,1,0:T(8,128)(2,1)} async-done(((bf16[32,40,128]{2,1,0:T(8,128)(2,1)}), bf16[32,40,128]{2,1,0:T(8,128)(2,1)}, u32[]{:S(2)}, u32[]{:S(2)}) %all-to-all-start) | async-done | bytes 327712 | tf_op jit(solution)/shard_map/all_to_all | solution.py:51
  65.3 445.1 %while.19 = (s32[]{:T(128)}, bf16[11,512,64]{1,2,0:T(8,128)(2,1)}, s32[11]{0:T(128)S(1)}, s32[]{:T(128)}, s32[1280]{0:T(1024)S(1)}, /*index=5*/s32[]{:T(128)}, p...) while((s32[]{:T(128)}, bf16[11,512,64]{1,2,0:T(8,128)(2,1)}, s32[11]{0:T(128)S(1)}, s32[]{:T(128)}, ...), condition=%wide.region_2.3_spmd, body=%wide.region_1.2_spmd.sunk | while | flops 183508736 | bytes 7038630 | solution.py:67
  68.3 35.9 %fusion.39 = (bf16[512,1280]{1,0:T(8,128)(2,1)S(1)}, bf16[512,1280]{1,0:T(8,128)(2,1)S(1)}) fusion(f32[]{:T(128)} %get-tuple-element.217, s32[]{:T(128)} %get-tuple-element.215, s32[1280]{0:T(1024)S(1)} %get-tuple-element.214, s32[512]{0:T(512)S(1)} %iota_add_fusion.3, f32[1280]{0:T(1024)S(1)} %select_select_fusion.2, ...), kind=kLoop, calls=%fused_computation.3.clone.1 | loop fusion | flops 10485760 | bytes 2634249 | tf_op jit(solution)/shard_map/while/body/eval_jaxpr/while/body/eval_jaxpr/convert_element_type | solution.py:25
  104.2 1.6 fusion.40
  108.8 35.9 %fusion.39 = (bf16[512,1280]{1,0:T(8,128)(2,1)S(1)}, bf16[512,1280]{1,0:T(8,128)(2,1)S(1)}) fusion(f32[]{:T(128)} %get-tuple-element.217, s32[]{:T(128)} %get-tuple-element.215, s32[1280]{0:T(1024)S(1)} %get-tuple-element.214, s32[512]{0:T(512)S(1)} %iota_add_fusion.3, f32[1280]{0:T(1024)S(1)} %select_select_fusion.2, ...), kind=kLoop, calls=%fused_computation.3.clone.1 | loop fusion | flops 10485760 | bytes 2634249 | tf_op jit(solution)/shard_map/while/body/eval_jaxpr/while/body/eval_jaxpr/convert_element_type | solution.py:25
  144.6 1.6 fusion.40
  149.2 35.9 %fusion.39 = (bf16[512,1280]{1,0:T(8,128)(2,1)S(1)}, bf16[512,1280]{1,0:T(8,128)(2,1)S(1)}) fusion(f32[]{:T(128)} %get-tuple-element.217, s32[]{:T(128)} %get-tuple-element.215, s32[1280]{0:T(1024)S(1)} %get-tuple-element.214, s32[512]{0:T(512)S(1)} %iota_add_fusion.3, f32[1280]{0:T(1024)S(1)} %select_select_fusion.2, ...), kind=kLoop, calls=%fused_computation.3.clone.1 | loop fusion | flops 10485760 | bytes 2634249 | tf_op jit(solution)/shard_map/while/body/eval_jaxpr/while/body/eval_jaxpr/convert_element_type | solution.py:25
  185.1 1.6 fusion.40
  189.7 35.9 %fusion.39 = (bf16[512,1280]{1,0:T(8,128)(2,1)S(1)}, bf16[512,1280]{1,0:T(8,128)(2,1)S(1)}) fusion(f32[]{:T(128)} %get-tuple-element.217, s32[]{:T(128)} %get-tuple-element.215, s32[1280]{0:T(1024)S(1)} %get-tuple-element.214, s32[512]{0:T(512)S(1)} %iota_add_fusion.3, f32[1280]{0:T(1024)S(1)} %select_select_fusion.2, ...), kind=kLoop, calls=%fused_computation.3.clone.1 | loop fusion | flops 10485760 | bytes 2634249 | tf_op jit(solution)/shard_map/while/body/eval_jaxpr/while/body/eval_jaxpr/convert_element_type | solution.py:25
  225.6 1.6 fusion.40
  230.1 35.9 %fusion.39 = (bf16[512,1280]{1,0:T(8,128)(2,1)S(1)}, bf16[512,1280]{1,0:T(8,128)(2,1)S(1)}) fusion(f32[]{:T(128)} %get-tuple-element.217, s32[]{:T(128)} %get-tuple-element.215, s32[1280]{0:T(1024)S(1)} %get-tuple-element.214, s32[512]{0:T(512)S(1)} %iota_add_fusion.3, f32[1280]{0:T(1024)S(1)} %select_select_fusion.2, ...), kind=kLoop, calls=%fused_computation.3.clone.1 | loop fusion | flops 10485760 | bytes 2634249 | tf_op jit(solution)/shard_map/while/body/eval_jaxpr/while/body/eval_jaxpr/convert_element_type | solution.py:25
  266.0 1.6 fusion.40
  270.6 35.9 %fusion.39 = (bf16[512,1280]{1,0:T(8,128)(2,1)S(1)}, bf16[512,1280]{1,0:T(8,128)(2,1)S(1)}) fusion(f32[]{:T(128)} %get-tuple-element.217, s32[]{:T(128)} %get-tuple-element.215, s32[1280]{0:T(1024)S(1)} %get-tuple-element.214, s32[512]{0:T(512)S(1)} %iota_add_fusion.3, f32[1280]{0:T(1024)S(1)} %select_select_fusion.2, ...), kind=kLoop, calls=%fused_computation.3.clone.1 | loop fusion | flops 10485760 | bytes 2634249 | tf_op jit(solution)/shard_map/while/body/eval_jaxpr/while/body/eval_jaxpr/convert_element_type | solution.py:25
  306.5 1.6 fusion.40
  311.1 35.9 %fusion.39 = (bf16[512,1280]{1,0:T(8,128)(2,1)S(1)}, bf16[512,1280]{1,0:T(8,128)(2,1)S(1)}) fusion(f32[]{:T(128)} %get-tuple-element.217, s32[]{:T(128)} %get-tuple-element.215, s32[1280]{0:T(1024)S(1)} %get-tuple-element.214, s32[512]{0:T(512)S(1)} %iota_add_fusion.3, f32[1280]{0:T(1024)S(1)} %select_select_fusion.2, ...), kind=kLoop, calls=%fused_computation.3.clone.1 | loop fusion | flops 10485760 | bytes 2634249 | tf_op jit(solution)/shard_map/while/body/eval_jaxpr/while/body/eval_jaxpr/convert_element_type | solution.py:25
  351.5 35.9 %fusion.39 = (bf16[512,1280]{1,0:T(8,128)(2,1)S(1)}, bf16[512,1280]{1,0:T(8,128)(2,1)S(1)}) fusion(f32[]{:T(128)} %get-tuple-element.217, s32[]{:T(128)} %get-tuple-element.215, s32[1280]{0:T(1024)S(1)} %get-tuple-element.214, s32[512]{0:T(512)S(1)} %iota_add_fusion.3, f32[1280]{0:T(1024)S(1)} %select_select_fusion.2, ...), kind=kLoop, calls=%fused_computation.3.clone.1 | loop fusion | flops 10485760 | bytes 2634249 | tf_op jit(solution)/shard_map/while/body/eval_jaxpr/while/body/eval_jaxpr/convert_element_type | solution.py:25
  392.0 35.9 %fusion.39 = (bf16[512,1280]{1,0:T(8,128)(2,1)S(1)}, bf16[512,1280]{1,0:T(8,128)(2,1)S(1)}) fusion(f32[]{:T(128)} %get-tuple-element.217, s32[]{:T(128)} %get-tuple-element.215, s32[1280]{0:T(1024)S(1)} %get-tuple-element.214, s32[512]{0:T(512)S(1)} %iota_add_fusion.3, f32[1280]{0:T(1024)S(1)} %select_select_fusion.2, ...), kind=kLoop, calls=%fused_computation.3.clone.1 | loop fusion | flops 10485760 | bytes 2634249 | tf_op jit(solution)/shard_map/while/body/eval_jaxpr/while/body/eval_jaxpr/convert_element_type | solution.py:25
  432.5 35.9 %fusion.39 = (bf16[512,1280]{1,0:T(8,128)(2,1)S(1)}, bf16[512,1280]{1,0:T(8,128)(2,1)S(1)}) fusion(f32[]{:T(128)} %get-tuple-element.217, s32[]{:T(128)} %get-tuple-element.215, s32[1280]{0:T(1024)S(1)} %get-tuple-element.214, s32[512]{0:T(512)S(1)} %iota_add_fusion.3, f32[1280]{0:T(1024)S(1)} %select_select_fusion.2, ...), kind=kLoop, calls=%fused_computation.3.clone.1 | loop fusion | flops 10485760 | bytes 2634249 | tf_op jit(solution)/shard_map/while/body/eval_jaxpr/while/body/eval_jaxpr/convert_element_type | solution.py:25
  472.9 35.9 %fusion.39 = (bf16[512,1280]{1,0:T(8,128)(2,1)S(1)}, bf16[512,1280]{1,0:T(8,128)(2,1)S(1)}) fusion(f32[]{:T(128)} %get-tuple-element.217, s32[]{:T(128)} %get-tuple-element.215, s32[1280]{0:T(1024)S(1)} %get-tuple-element.214, s32[512]{0:T(512)S(1)} %iota_add_fusion.3, f32[1280]{0:T(1024)S(1)} %select_select_fusion.2, ...), kind=kLoop, calls=%fused_computation.3.clone.1 | loop fusion | flops 10485760 | bytes 2634249 | tf_op jit(solution)/shard_map/while/body/eval_jaxpr/while/body/eval_jaxpr/convert_element_type | solution.py:25
  508.8 1.6 fusion.40
  510.4 2.4 copy.13
  512.8 9.0 %reshape.68 = bf16[1,5632,64]{2,0,1:T(2,128)(2,1)} reshape(bf16[11,512,64]{2,1,0:T(8,128)(2,1)} %copy.13) | data formatting | bytes 1441792 | tf_op jit(solution)/shard_map/while/body/eval_jaxpr/convert_element_type | solution.py:67
  522.3 32.7 %reduce = bf16[5632,64]{1,0:T(8,128)(2,1)} reduce(bf16[5632,1,64]{2,1,0:T(2,128)(2,1)} %bitcast.20, bf16[]{:T(256)} %broadcast.100), dimensions={1}, to_apply=%bitcast.10.reduce_sub_computation | reduce | bytes 1441794
  555.1 2.8 reshape.70
  557.9 18.0 %all_to_all.21 = bf16[32,2,5632]{2,1,0:T(2,128)(2,1)} all-to-all(bf16[32,2,5632]{2,1,0:T(2,128)(2,1)} %reshape.70), channel_id=1, replica_groups=mesh['wave'=32,'lat'=4] {'wave'}, dimensions={0} | all-to-all | bytes 1441792 | tf_op jit(solution)/shard_map/all_to_all | solution.py:70
  575.8 8.6 %reshape.71 = bf16[5632,1,64]{2,1,0:T(2,128)(2,1)} reshape(bf16[32,2,5632]{2,1,0:T(2,128)(2,1)} %all_to_all.21) | data formatting | bytes 1441792
  584.4 3.1 copy.17
  587.6 2.6 copy.12
  (87 shorter events, 44.4 us)
Async XLA Ops:
  6.5 1.9 copy-start
  6.5 37.9 %reduce-scatter.2.cloned.1.call-start = ((), (), s32[]{:S(2)}) async-start(), calls=%async_computation.3 | async-start | bytes 1638400 | tf_op jit(solution)/shard_map/reduce_scatter | solution.py:42
  15.0 38.4 %copy-start.3 = (s32[128]{0:T(128)S(1)}, s32[128]{0:T(128)}, u32[]{:S(2)}) copy-start(s32[128]{0:T(128)} %param.9) | copy-start | bytes 1540
  17.8 47.5 %copy-start.1 = (s32[1280]{0:T(1024)S(1)}, s32[1280]{0:T(1024)}, u32[]{:S(2)}) copy-start(s32[1280]{0:T(1024)} %param.8) | copy-start | bytes 15364
  44.4 18.7 %all-to-all-start = ((bf16[32,40,128]{2,1,0:T(8,128)(2,1)}), bf16[32,40,128]{2,1,0:T(8,128)(2,1)}, u32[]{:S(2)}, u32[]{:S(2)}) async-start(bf16[32,40,128]{2,1,0:T(8,128)(2,1)} %reduce-scatter.2.cloned.1.call-done), calls=%async_computation.1 | async-start | bytes 655360 | tf_op jit(solution)/shard_map/all_to_all | solution.py:51
  65.3 38.9 %copy-start.2 = (bf16[2560,64]{1,0:T(8,128)(2,1)S(1)}, bf16[2560,64]{1,0:T(8,128)(2,1)}, u32[]{:S(2)}) copy-start(bf16[2560,64]{1,0:T(8,128)(2,1)} %get-tuple-element.218) | copy-start | bytes 983044 | tf_op jit(solution)/shard_map/while/body/eval_jaxpr/while
  105.7 38.9 %copy-start.2 = (bf16[2560,64]{1,0:T(8,128)(2,1)S(1)}, bf16[2560,64]{1,0:T(8,128)(2,1)}, u32[]{:S(2)}) copy-start(bf16[2560,64]{1,0:T(8,128)(2,1)} %get-tuple-element.218) | copy-start | bytes 983044 | tf_op jit(solution)/shard_map/while/body/eval_jaxpr/while
  146.2 38.9 %copy-start.2 = (bf16[2560,64]{1,0:T(8,128)(2,1)S(1)}, bf16[2560,64]{1,0:T(8,128)(2,1)}, u32[]{:S(2)}) copy-start(bf16[2560,64]{1,0:T(8,128)(2,1)} %get-tuple-element.218) | copy-start | bytes 983044 | tf_op jit(solution)/shard_map/while/body/eval_jaxpr/while
  186.7 38.9 %copy-start.2 = (bf16[2560,64]{1,0:T(8,128)(2,1)S(1)}, bf16[2560,64]{1,0:T(8,128)(2,1)}, u32[]{:S(2)}) copy-start(bf16[2560,64]{1,0:T(8,128)(2,1)} %get-tuple-element.218) | copy-start | bytes 983044 | tf_op jit(solution)/shard_map/while/body/eval_jaxpr/while
  227.1 38.9 %copy-start.2 = (bf16[2560,64]{1,0:T(8,128)(2,1)S(1)}, bf16[2560,64]{1,0:T(8,128)(2,1)}, u32[]{:S(2)}) copy-start(bf16[2560,64]{1,0:T(8,128)(2,1)} %get-tuple-element.218) | copy-start | bytes 983044 | tf_op jit(solution)/shard_map/while/body/eval_jaxpr/while
  267.6 38.9 %copy-start.2 = (bf16[2560,64]{1,0:T(8,128)(2,1)S(1)}, bf16[2560,64]{1,0:T(8,128)(2,1)}, u32[]{:S(2)}) copy-start(bf16[2560,64]{1,0:T(8,128)(2,1)} %get-tuple-element.218) | copy-start | bytes 983044 | tf_op jit(solution)/shard_map/while/body/eval_jaxpr/while
  308.1 38.9 %copy-start.2 = (bf16[2560,64]{1,0:T(8,128)(2,1)S(1)}, bf16[2560,64]{1,0:T(8,128)(2,1)}, u32[]{:S(2)}) copy-start(bf16[2560,64]{1,0:T(8,128)(2,1)} %get-tuple-element.218) | copy-start | bytes 983044 | tf_op jit(solution)/shard_map/while/body/eval_jaxpr/while
  348.5 38.9 %copy-start.2 = (bf16[2560,64]{1,0:T(8,128)(2,1)S(1)}, bf16[2560,64]{1,0:T(8,128)(2,1)}, u32[]{:S(2)}) copy-start(bf16[2560,64]{1,0:T(8,128)(2,1)} %get-tuple-element.218) | copy-start | bytes 983044 | tf_op jit(solution)/shard_map/while/body/eval_jaxpr/while
  389.0 38.9 %copy-start.2 = (bf16[2560,64]{1,0:T(8,128)(2,1)S(1)}, bf16[2560,64]{1,0:T(8,128)(2,1)}, u32[]{:S(2)}) copy-start(bf16[2560,64]{1,0:T(8,128)(2,1)} %get-tuple-element.218) | copy-start | bytes 983044 | tf_op jit(solution)/shard_map/while/body/eval_jaxpr/while
  429.4 38.9 %copy-start.2 = (bf16[2560,64]{1,0:T(8,128)(2,1)S(1)}, bf16[2560,64]{1,0:T(8,128)(2,1)}, u32[]{:S(2)}) copy-start(bf16[2560,64]{1,0:T(8,128)(2,1)} %get-tuple-element.218) | copy-start | bytes 983044 | tf_op jit(solution)/shard_map/while/body/eval_jaxpr/while
  469.9 38.9 %copy-start.2 = (bf16[2560,64]{1,0:T(8,128)(2,1)S(1)}, bf16[2560,64]{1,0:T(8,128)(2,1)}, u32[]{:S(2)}) copy-start(bf16[2560,64]{1,0:T(8,128)(2,1)} %get-tuple-element.218) | copy-start | bytes 983044 | tf_op jit(solution)/shard_map/while/body/eval_jaxpr/while
Sparse Core Ops, SparseCore 0:
  17.9 26.4 reduce-scatter.1
where the time goes:
time: 599 us; the launch traced here: 597 us
  other arithmetic  455 us (76%)
  local copies, waits for them, and re-layouts  41.7 us (7%)
  waiting for transfers between devices  34 us (6%)
  matrix products  23.6 us (4%)
  blocking collectives  18 us (3%)
  between operations  15.1 us (3%)
  starting transfers between devices  8.96 us (1%)
    convert_element_type x11, other arithmetic, lon_block_table(): cosine_part = (scales * jnp.cos(angles)).astype(jnp.bfloat16)  395 us
    unnamed x1, other arithmetic  32.7 us
    reduce_scatter x1, waiting for transfers between devices, local(): lax.psum_scatter(jnp.einsum('sjw,sjc->wsc', legendre, masked, preferred_e...  26.6 us
    all_to_all x1, blocking collectives, local(): lax.all_to_all(rows_grid, 'wave', split_axis=1, concat_axis=0, tiled=True)  18 us
    dot_general x11, matrix products, compute_block(): return jnp.dot(table, stacked, preferred_element_type=jnp.float32)  17.1 us
    unnamed x10, local copies, waits for them, and re-layouts  16 us
    lt x11, other arithmetic, lon_block_table(): scales = jnp.where((k_index < row_lons)[:, None], weights[None, :], 0.0)  12.9 us
  transfers between devices with their start and end apart: 2, of which 2 were waited for; matrix products, arithmetic and copies ran while one was open for 0% of the time, Pallas kernels for 0%

commit v1 on v0

v1 whole, which is shorter than its diff:
```python
import jax
import jax.numpy as jnp
from jax import lax
from jax.experimental import pallas as pl
from jax.experimental.pallas import tpu as pltpu
from jax.sharding import PartitionSpec as P

M = 1280
F = 64
NLW = 128
NLAT = 2560
STRIDE = 20
NLONP = 5632
N_WAVE = 32
N_LAT = 4

SLOTS = M // N_WAVE
DEPTH = M // N_LAT
BAND = NLW // N_LAT
LONS = NLONP // N_WAVE
HALF = LONS // 2
LANES = 128
QUADS = N_WAVE // 4
GROUPS = ((0, 24), (24, 16))

COS_TERMS = (
    0.999999009718151, -19.738932854525416, 64.92691787698224,
    -85.24978872544477, 58.68039930519758, -20.879193249375327,
)
SIN_TERMS = (
    6.283184816484557, -41.34156560570182, 81.59907809153451,
    -76.60361308658534, 41.288123420059144, -12.375788874464046,
)


def cos_sin(product, two_lons, inverse):
    turns = jnp.floor(product * inverse + 0.5)
    u = (product - turns * two_lons) * inverse
    z = u * u
    c = jnp.full_like(z, COS_TERMS[-1])
    for term in COS_TERMS[-2::-1]:
        c = c * z + term
    s = jnp.full_like(z, SIN_TERMS[-1])
    for term in SIN_TERMS[-2::-1]:
        s = s * z + term
    return c, s * u


def kernel(waves_s, lons_s, waves_v, spectra, legendre, raw, *scratch):
    names = iter(scratch)
    spec, leg, partial = next(names), next(names), next(names)
    bands, from_dn, from_up, sum_dn, sum_up, mine, got, coef, table = (
        [next(names) for _ in GROUPS] for _ in range(9)
    )
    acc, out, m_nat, m_grp, c0, s0, c1, s1 = (next(names) for _ in range(8))
    in_sem, y_send, y_recv, a_send, a_recv, o_send, o_recv, own_sem = names

    me = lax.axis_index("wave")
    lat = lax.axis_index("lat")
    up = lax.rem(lat + 1, N_LAT)
    dn = lax.rem(lat + N_LAT - 1, N_LAT)
    opp = lax.rem(lat + 2, N_LAT)
    row = lat * BAND + me

    def most_lons(w):
        first = STRIDE * w + STRIDE - 1
        last = NLAT - 1 - STRIDE * w
        return 20 + 4 * jnp.minimum(first, last)

    def peer(step):
        return lax.rem(me + step, N_WAVE)

    def load(g, which):
        off, size = GROUPS[g]
        source, target = ((spectra, spec), (legendre, leg))[which]
        return pltpu.make_async_copy(
            source.at[pl.ds(off, size)], target.at[pl.ds(off, size)], in_sem.at[g, which]
        )

    for g in range(len(GROUPS)):
        for which in range(2):
            load(g, which).start()

    barrier = pltpu.get_barrier_semaphore()
    for other in (up, dn):
        pl.semaphore_signal(
            barrier, inc=1, device_id={"wave": me, "lat": other}, device_id_type=pl.DeviceIdType.MESH
        )

    def greet(step, carry):
        pl.semaphore_signal(
            barrier, inc=1, device_id={"wave": peer(step), "lat": lat},
            device_id_type=pl.DeviceIdType.MESH,
        )
        return carry

    lax.fori_loop(1, N_WAVE, greet, 0)

    def along_y(g, at, source, target, other):
        return pltpu.make_async_remote_copy(
            src_ref=source, dst_ref=target, send_sem=y_send.at[g, at], recv_sem=y_recv.at[g, at],
            device_id={"wave": me, "lat": other}, device_id_type=pl.DeviceIdType.MESH,
        )

    def y_copies(g):
        half = BAND // 2 * GROUPS[g][1]
        lo, hi = pl.ds(0, half), pl.ds(half, half)
        b = bands[g]
        return (
            along_y(g, 0, b.at[opp, lo], from_dn[g], up),
            along_y(g, 1, b.at[opp, hi], from_up[g], dn),
            along_y(g, 2, b.at[up, hi], sum_dn[g].at[hi], up),
            along_y(g, 3, b.at[dn, lo], sum_up[g].at[lo], dn),
            along_y(g, 4, b.at[up, lo], sum_dn[g].at[lo], up),
            along_y(g, 5, b.at[dn, hi], sum_up[g].at[hi], dn),
        )

    def legendre_sums(g):
        off, size = GROUPS[g]
        load(g, 0).wait()
        load(g, 1).wait()

        def slot(s, carry):
            live = M - waves_s[me * SLOTS + off + s] - lat * DEPTH
            offsets = lax.broadcasted_iota(jnp.int32, (DEPTH, LANES), 0)
            masked = jnp.where(offsets < live, spec[off + s].astype(jnp.float32), 0.0)
            partial[pl.ds(pl.multiple_of(s * NLW, NLW), NLW), :] = lax.dot_general(
                leg[off + s], masked.astype(jnp.bfloat16), (((0,), (0,)), ((), ())),
                preferred_element_type=jnp.float32,
            )
            return carry

        lax.fori_loop(0, size, slot, 0, unroll=4)

    def by_row(g, band):
        size = GROUPS[g][1]

        def pair(i, carry):
            first = band * BAND + 2 * i
            rows = [partial[pl.ds(first + j, size, stride=NLW), :] for j in range(2)]
            bands[g][band, pl.ds(pl.multiple_of(i * 2 * size, 2 * size), 2 * size), :] = (
                jnp.concatenate(rows, 0).astype(jnp.bfloat16)
            )
            return carry

        lax.fori_loop(0, BAND // 2, pair, 0, unroll=4)

    def merge(g, band, at, received):
        half = BAND // 2 * GROUPS[g][1]
        step = half // 4

        def part(i, carry):
            rows = pl.ds(pl.multiple_of(at * half + i * step, 32), step)
            other = pl.ds(pl.multiple_of(i * step, 32), step)
            total = bands[g][band, rows, :].astype(jnp.float32) + received[other, :].astype(jnp.float32)
            bands[g][band, rows, :] = total.astype(jnp.bfloat16)
            return carry

        lax.fori_loop(0, 4, part, 0)

    def total(g):
        size = GROUPS[g][1]

        def pair(i, carry):
            rows = pl.ds(pl.multiple_of(i * 2 * size, 2 * size), 2 * size)
            value = bands[g][lat, rows, :].astype(jnp.float32)
            value += sum_dn[g][rows, :].astype(jnp.float32)
            value += sum_up[g][rows, :].astype(jnp.float32)
            mine[g][2 * i] = value[:size].astype(jnp.bfloat16)
            mine[g][2 * i + 1] = value[size:].astype(jnp.bfloat16)
            return carry

        lax.fori_loop(0, BAND // 2, pair, 0, unroll=2)

    def to_row(g, other, sender):
        return pltpu.make_async_remote_copy(
            src_ref=mine[g].at[other], dst_ref=got[g].at[sender],
            send_sem=a_send.at[g, other], recv_sem=a_recv.at[g, sender],
            device_id={"wave": other, "lat": lat}, device_id_type=pl.DeviceIdType.MESH,
        )

    def send_rows(g):
        def one(step, carry):
            to_row(g, peer(step), me).start()
            return carry

        lax.fori_loop(1, N_WAVE, one, 0)
        got[g][me] = mine[g][me]

    def wait_rows(g):
        def one(step, carry):
            to_row(g, me, peer(step)).wait_recv()
            return carry

        lax.fori_loop(1, N_WAVE, one, 0)

    def tables():
        lons = lons_s[row].astype(jnp.float32)
        two = 2.0 * lons
        inverse = 1.0 / jnp.full((8, LANES), two, jnp.float32)

        def spread(r, carry):
            line = waves_v[pl.ds(r, 1), :].astype(jnp.float32)
            m_nat[pl.ds(pl.multiple_of(r * LANES, LANES), LANES), :] = jnp.transpose(
                jnp.broadcast_to(line, (LANES, LANES))
            )
            return carry

        lax.fori_loop(0, M // LANES, spread, 0)

        def regroup(v, carry):
            for off, size in GROUPS:
                m_grp[pl.ds(pl.multiple_of(N_WAVE * off + v * size, 8), size), :] = m_nat[
                    pl.ds(pl.multiple_of(v * SLOTS + off, 8), size), :
                ]
            return carry

        lax.fori_loop(0, N_WAVE, regroup, 0)

        lane = lax.broadcasted_iota(jnp.int32, (8, LANES), 1)
        first = jnp.where(lane < F, LONS - 1.0, 3.0 * LONS - 1.0).astype(jnp.float32)

        def phases(i, carry):
            for j in range(4):
                rows = pl.ds(pl.multiple_of(i * 32 + j * 8, 8), 8)
                m = m_grp[rows, :]
                weight = jnp.where(m == 0.0, 1.0, jnp.where(2.0 * m < lons, 2.0, 0.0))
                c, s = cos_sin(m * first, two, inverse)
                c0[rows, :] = weight * c
                s0[rows, :] = weight * s
                c, s = cos_sin(m * (4.0 * LONS), two, inverse)
                c1[rows, :] = c
                s1[rows, :] = s
            return carry

        lax.fori_loop(0, M // 32, phases, 0)

        for g, (off, size) in enumerate(GROUPS):
            depth = N_WAVE * size

            def columns(i, carry, g=g, off=off, depth=depth):
                base = pl.multiple_of(N_WAVE * off + i * LANES, LANES)
                m = jnp.transpose(m_grp[pl.ds(base, LANES), :])[0:8, :]
                for r in range(0, LONS, 16):
                    parts = []
                    for h in range(2):
                        k = lax.broadcasted_iota(jnp.int32, (8, LANES), 0) + (r + 8 * h)
                        k = (2 * k - (LONS - 1)).astype(jnp.float32)
                        parts.append(cos_sin(m * k, two, inverse))
                    c = jnp.concatenate([p[0] for p in parts], 0)
                    s = jnp.concatenate([p[1] for p in parts], 0)
                    at = pl.multiple_of(i * LANES, LANES)
                    table[g][r : r + 16, pl.ds(at, LANES)] = c.astype(jnp.bfloat16)
                    at = pl.multiple_of(depth + i * LANES, LANES)
                    table[g][r : r + 16, pl.ds(at, LANES)] = (-s).astype(jnp.bfloat16)
                return carry

            lax.fori_loop(0, depth // LANES, columns, 0)

    def rotate(g):
        off, size = GROUPS[g]
        depth = N_WAVE * size

        def pair(i, carry):
            value = jnp.concatenate(
                [got[g][2 * i + j].astype(jnp.float32) for j in range(2)], 0
            )
            swapped = pltpu.roll(value, F, 1)
            lane = lax.broadcasted_iota(jnp.int32, value.shape, 1)
            real = jnp.where(lane < F, value, swapped)
            imag = jnp.where(lane < F, swapped, value)
            rows = pl.ds(pl.multiple_of(N_WAVE * off + i * 2 * size, 16), 2 * size)
            c, s = c0[rows, :], s0[rows, :]
            a, b = real * c - imag * s, real * s + imag * c
            c, s = c1[rows, :], s1[rows, :]
            at = pl.multiple_of(i * 2 * size, 16)
            for p in range(2 * QUADS - 1):
                columns = slice(LANES * (p % 2), LANES * (p % 2) + LANES)
                coef[g][p // 2, pl.ds(at, 2 * size), columns] = a.astype(jnp.bfloat16)
                coef[g][p // 2, pl.ds(depth + at, 2 * size), columns] = b.astype(jnp.bfloat16)
                if p < 2 * QUADS - 2:
                    a, b = a * c - b * s, a * s + b * c
            zero = jnp.zeros((2 * size, LANES), jnp.bfloat16)
            coef[g][QUADS - 1, pl.ds(at, 2 * size), LANES:] = zero
            coef[g][QUADS - 1, pl.ds(depth + at, 2 * size), LANES:] = zero
            return carry

        lax.fori_loop(0, N_WAVE // 2, pair, 0)

    def product(g, quad):
        return jnp.dot(table[g][...], coef[g][quad], preferred_element_type=jnp.float32)

    def to_owner(other, sender):
        return pltpu.make_async_remote_copy(
            src_ref=out.at[other], dst_ref=raw.at[sender],
            send_sem=o_send.at[other], recv_sem=o_recv.at[sender],
            device_id={"wave": other, "lat": lat}, device_id_type=pl.DeviceIdType.MESH,
        )

    def keep():
        return pltpu.make_async_copy(out.at[me], raw.at[me], own_sem)

    limit = most_lons(row)
    last = len(GROUPS) - 1

    copies = [y_copies(g) for g in range(len(GROUPS))]
    legendre_sums(0)
    by_row(0, opp)
    pl.semaphore_wait(barrier, N_WAVE + 1)
    copies[0][0].start()
    copies[0][1].start()
    by_row(0, up)
    copies[0][2].start()
    by_row(0, dn)
    copies[0][3].start()
    by_row(0, lat)
    legendre_sums(1)
    copies[0][0].wait_recv()
    merge(0, up, 0, from_dn[0])
    copies[0][4].start()
    copies[0][1].wait_recv()
    merge(0, dn, 1, from_up[0])
    copies[0][5].start()
    by_row(1, opp)
    copies[1][0].start()
    copies[1][1].start()
    by_row(1, up)
    copies[1][2].start()
    by_row(1, dn)
    copies[1][3].start()
    by_row(1, lat)
    tables()
    copies[1][0].wait_recv()
    merge(1, up, 0, from_dn[1])
    copies[1][4].start()
    copies[1][1].wait_recv()
    merge(1, dn, 1, from_up[1])
    copies[1][5].start()

    for at in range(2, 6):
        copies[0][at].wait_recv()
    total(0)
    send_rows(0)
    for at in range(2, 6):
        copies[1][at].wait_recv()
    total(1)
    send_rows(1)

    wait_rows(0)
    rotate(0)

    def early(quad, carry):
        acc[quad] = product(0, quad)
        return carry

    lax.fori_loop(0, QUADS, early, 0)
    wait_rows(1)
    rotate(1)

    def late(step, carry):
        quad = lax.rem(me // 4 + step, QUADS)
        value = acc[quad] + product(1, quad)
        lane = lax.broadcasted_iota(jnp.int32, (HALF, LANES), 1)
        for p in range(2):
            top = value[:HALF, LANES * p : LANES * (p + 1)]
            bottom = value[HALF:, LANES * p : LANES * (p + 1)]
            even = jnp.where(lane < F, top, pltpu.roll(bottom, F, 1))
            odd = jnp.where(lane < F, pltpu.roll(top, F, 1), bottom)
            out[quad * 4 + 2 * p] = even.astype(jnp.bfloat16)
            out[quad * 4 + 2 * p + 1] = odd.astype(jnp.bfloat16)
        for j in range(4):
            other = quad * 4 + j

            @pl.when((other != me) & (other * LONS < limit))
            def _():
                to_owner(other, me).start()

        return carry

    lax.fori_loop(0, QUADS, late, 0)

    @pl.when(me * LONS < limit)
    def _():
        keep().start()

    def arrived(step, carry):
        sender = peer(step)

        @pl.when(me * LONS < most_lons(lat * BAND + sender))
        def _():
            to_owner(me, sender).wait_recv()

        other = peer(step)

        @pl.when(other * LONS < limit)
        def _():
            to_owner(other, me).wait_send()

        for g in range(len(GROUPS)):
            to_row(g, other, me).wait_send()
        return carry

    lax.fori_loop(1, N_WAVE, arrived, 0)

    @pl.when(me * LONS < limit)
    def _():
        keep().wait()

    for g in range(len(GROUPS)):
        for copy in copies[g]:
            copy.wait_send()


def local(spectra, legendre, wave_list, cycle_lons):
    bf16, f32 = jnp.bfloat16, jnp.float32
    sizes = [size for _, size in GROUPS]
    scratch = [
        pltpu.VMEM((SLOTS, DEPTH, LANES), bf16),
        pltpu.VMEM((SLOTS, DEPTH, LANES), bf16),
        pltpu.VMEM((max(sizes) * NLW, LANES), f32),
    ]
    scratch += [pltpu.VMEM((N_LAT, BAND * n, LANES), bf16) for n in sizes]
    for rows in (BAND // 2, BAND // 2, BAND, BAND):
        scratch += [pltpu.VMEM((rows * n, LANES), bf16) for n in sizes]
    scratch += [pltpu.VMEM((BAND, n, LANES), bf16) for n in sizes]
    scratch += [pltpu.VMEM((N_WAVE, n, LANES), bf16) for n in sizes]
    scratch += [pltpu.VMEM((QUADS, 2 * N_WAVE * n, 2 * LANES), bf16) for n in sizes]
    scratch += [pltpu.VMEM((LONS, 2 * N_WAVE * n), bf16) for n in sizes]
    scratch += [pltpu.VMEM((QUADS, LONS, 2 * LANES), f32), pltpu.VMEM((N_WAVE, HALF, LANES), bf16)]
    scratch += [pltpu.VMEM((M, LANES), f32) for _ in range(6)]
    dma = pltpu.SemaphoreType.DMA
    count = len(GROUPS)
    scratch += [dma((count, 2)), dma((count, 6)), dma((count, 6)), dma((count, N_WAVE))]
    scratch += [dma((count, N_WAVE)), dma((N_WAVE,)), dma((N_WAVE,)), dma]

    raw = pl.pallas_call(
        kernel,
        out_shape=jax.ShapeDtypeStruct((BAND, HALF, LANES), bf16),
        in_specs=[
            pl.BlockSpec(memory_space=pltpu.SMEM),
            pl.BlockSpec(memory_space=pltpu.SMEM),
            pl.BlockSpec(memory_space=pltpu.VMEM),
            pl.BlockSpec(memory_space=pl.ANY),
            pl.BlockSpec(memory_space=pl.ANY),
        ],
        out_specs=pl.BlockSpec(memory_space=pl.ANY),
        scratch_shapes=scratch,
        compiler_params=pltpu.CompilerParams(
            collective_id=0, has_side_effects=True, vmem_limit_bytes=56 * 2**20
        ),
    )(wave_list, cycle_lons, wave_list.reshape(M // LANES, LANES), spectra, legendre)

    first = lax.axis_index("lat") * BAND
    band_lons = lax.dynamic_slice_in_dim(cycle_lons, first, BAND)
    k = lax.axis_index("wave") * LONS + jnp.arange(LONS, dtype=jnp.int32)
    rows = jnp.concatenate([raw[:, :, :F], raw[:, :, F:]], 1)
    return jnp.where((k[None, :] < band_lons[:, None])[:, :, None], rows, jnp.zeros_like(rows))


def solution(mesh):
    in_specs = (P("wave", "lat", None), P("wave", "lat", None), P(), P())
    out_specs = P("lat", "wave", None)
    return jax.shard_map(local, mesh=mesh, in_specs=in_specs, out_specs=out_specs, check_vma=False)
```

time: 599 us -> 56.2 us (0.09)
  other arithmetic: 455 us -> 1.15 us
  Pallas kernels: 0 us -> 50.9 us
  local copies, waits for them, and re-layouts: 41.7 us -> 3.9 us
  waiting for transfers between devices: 34 us -> 0 us
  matrix products: 23.6 us -> 0 us
  blocking collectives: 18 us -> 0 us
  between operations: 15.1 us -> 0.02 us
  starting transfers between devices: 8.96 us -> 0 us
    convert_element_type x11 -> x0, other arithmetic: 395 us -> none  [lon_block_table(): cosine_part = (scales * jnp.cos(angles)).astype(jnp.bfloat16)]
    pallas_call x0 -> x1, Pallas kernels: none -> 50.9 us  [local(): pl.pallas_call(kernel, out_shape=jax.ShapeDtypeStruct((BAND, HALF, LANES)...]
    unnamed x1 -> x0, other arithmetic: 32.7 us -> none
    reduce_scatter x1 -> x0, waiting for transfers between devices: 26.6 us -> none  [local(): lax.psum_scatter(jnp.einsum('sjw,sjc->wsc', legendre, masked, preferred_e...]
    dot_general x12 -> x0, matrix products: 23.6 us -> none  [the longest x11 17.1 us: compute_block(): return jnp.dot(table, stacked, preferred_element_type=jnp.float32)]
    all_to_all x1 -> x0, blocking collectives: 18 us -> none  [local(): lax.all_to_all(rows_grid, 'wave', split_axis=1, concat_axis=0, tiled=True)]
    unnamed x10 -> x0, local copies, waits for them, and re-layouts: 16 us -> none
    convert_element_type x3 -> x0, local copies, waits for them, and re-layouts: 14.2 us -> none  [the longest x2 11.5 us: one_row(): lax.map(lon_block, starts).reshape(slot_total, F).astype(jnp.bfloat16)]
  transfers between devices with their start and end apart: 2 -> 0, of which waited for: 2 -> 0; matrix products, arithmetic and copies ran while one was open for 0% -> 0% of each run, Pallas kernels for 0% -> 0%
where the time goes in v1:
time: 56.2 us; the launch traced here: 56 us
  Pallas kernels  50.9 us (91%)
  local copies, waits for them, and re-layouts  3.9 us (7%)
  other arithmetic  1.15 us (2%)
    pallas_call x1, Pallas kernels, local(): pl.pallas_call(kernel, out_shape=jax.ShapeDtypeStruct((BAND, HALF, LANES)...  50.9 us
    slice x1, local copies, waits for them, and re-layouts, local(): rows = jnp.concatenate([raw[:, :, :F], raw[:, :, F:]], 1)  1.61 us
    select_n x1, local copies, waits for them, and re-layouts, local(): jnp.where((k[None, :] < band_lons[:, None])[:, :, None], rows, jnp.zeros_...  1.57 us

profile of v1, /device:TPU:1, one launch (start us, length us, event | category | flops | bytes accessed | tf_op | source)
XLA Modules:
  0.0 56.0 jit_solution(11879678174699045937)
XLA Ops:
  0.0 0.7 %dynamic_slice.3 = s32[32]{0:T(128)S(1)} dynamic-slice(s32[128]{0:T(128)} %lons_s.1, s32[]{:T(128)S(6)} %select_n.7), dynamic_slice_sizes={32} | dynamic-slice | bytes 260 | tf_op jit(solution)/shard_map/dynamic_slice | solution.py:454
  0.7 0.1 broadcast_compare_fusion
  0.8 50.9 %shard_map.46 = bf16[32,88,128]{2,1,0:T(8,128)(2,1)} custom-call(s32[1280]{0:T(1024)} %waves_s.1, s32[128]{0:T(128)} %lons_s.1, s32[10,128]{1,0:T(8,128)} %bitcast.1, bf16[40,320,128]{2,1,0:T(8,128)(2,1)} %spectra.1, bf16[40,320,128]{2,1,0:T(8,128)(2,1)} %legendre.1), custom_call_target="tpu_custom_call" | custom-call | tf_op jit(solution)/shard_map/pallas_call | solution.py:436
  51.7 1.6 %fusion = (bf16[32,88,64]{2,1,0:T(8,128)(2,1)S(1)}, bf16[32,88,64]{2,1,0:T(8,128)(2,1)S(1)}) fusion(bf16[32,88,128]{2,1,0:T(8,128)(2,1)} %shard_map.46), kind=kLoop, calls=%fused_computation.3 | loop fusion | bytes 1441792 | tf_op jit(solution)/shard_map/slice | solution.py:456
  53.3 1.1 %maximum_select_fusion = bf16[32,176,64]{2,1,0:T(8,128)(2,1)S(1)} fusion(bf16[32,88,64]{2,1,0:T(8,128)(2,1)S(1)} %get-tuple-element.6, bf16[32,88,64]{2,1,0:T(8,128)(2,1)S(1)} %get-tuple-element.5, pred[32,176]{1,0:T(8,128)(4,1)S(1)} %broadcast_compare_fusion), kind=kLoop, calls=%fused_computation | loop fusion | flops 1802240 | bytes 1447424 | tf_op jit(solution)/shard_map/jit(_where)/select_n | solution.py:457
  54.4 1.6 %copy.5 = bf16[32,176,64]{1,2,0:T(8,128)(2,1)} copy(bf16[32,176,64]{2,1,0:T(8,128)(2,1)S(1)} %maximum_select_fusion) | data formatting | bytes 1441792 | tf_op jit(solution)/shard_map/jit(_where)/select_n | solution.py:457
  (1 shorter events, 0.0 us)

commit v2 on v1

--- a/solution.py
+++ b/solution.py
@@ -20,7 +20,8 @@
 LONS = NLONP // N_WAVE
 HALF = LONS // 2
 LANES = 128
-QUADS = N_WAVE // 4
+BLOCK = 2 * LONS
+QUADS = N_WAVE // 8
 GROUPS = ((0, 24), (24, 16))
 
 COS_TERMS = (
@@ -46,14 +47,14 @@
     return c, s * u
 
 
-def kernel(waves_s, lons_s, waves_v, spectra, legendre, raw, *scratch):
+def kernel(waves_s, lons_s, waves_v, spectra, legendre, grid, *scratch):
     names = iter(scratch)
     spec, leg, partial = next(names), next(names), next(names)
     bands, from_dn, from_up, sum_dn, sum_up, mine, got, coef, table = (
         [next(names) for _ in GROUPS] for _ in range(9)
     )
-    acc, out, m_nat, m_grp, c0, s0, c1, s1 = (next(names) for _ in range(8))
-    in_sem, y_send, y_recv, a_send, a_recv, o_send, o_recv, own_sem = names
+    acc, out, raw, turn, m_nat, m_grp, c0, s0, c1, s1 = (next(names) for _ in range(10))
+    in_sem, y_send, y_recv, a_send, a_recv, o_send, o_recv, own_sem, line_sem = names
 
     me = lax.axis_index("wave")
     lat = lax.axis_index("lat")
@@ -68,7 +69,7 @@
         return 20 + 4 * jnp.minimum(first, last)
 
     def peer(step):
-        return lax.rem(me + step, N_WAVE)
+        return jnp.bitwise_and(me + step, N_WAVE - 1)
 
     def load(g, which):
         off, size = GROUPS[g]
@@ -87,14 +88,28 @@
             barrier, inc=1, device_id={"wave": me, "lat": other}, device_id_type=pl.DeviceIdType.MESH
         )
 
-    def greet(step, carry):
+    def shifted(dx, dz, dcore):
+        x = jnp.bitwise_and(me // 8 + dx, 3)
+        z = jnp.bitwise_and(me // 2 + dz, 3)
+        return x * 8 + z * 2 + jnp.bitwise_xor(jnp.bitwise_and(me, 1), dcore)
+
+    plane = [(dx, 0, dcore) for dx in range(4) for dcore in range(2) if dx or dcore]
+    line = [(0, dz, 0) for dz in range(1, 4)]
+    for shift in plane + line:
         pl.semaphore_signal(
-            barrier, inc=1, device_id={"wave": peer(step), "lat": lat},
+            barrier, inc=1, device_id={"wave": shifted(*shift), "lat": lat},
             device_id_type=pl.DeviceIdType.MESH,
         )
-        return carry
-
-    lax.fori_loop(1, N_WAVE, greet, 0)
+
+    def tell():
+        for shift in line:
+            pl.semaphore_signal(
+                line_sem, inc=1, device_id={"wave": shifted(*shift), "lat": lat},
+                device_id_type=pl.DeviceIdType.MESH,
+            )
+
+    def hear():
+        pl.semaphore_wait(line_sem, len(line))
 
     def along_y(g, at, source, target, other):
         return pltpu.make_async_remote_copy(
@@ -175,29 +190,31 @@
     def to_row(g, other, sender):
         return pltpu.make_async_remote_copy(
             src_ref=mine[g].at[other], dst_ref=got[g].at[sender],
-            send_sem=a_send.at[g, other], recv_sem=a_recv.at[g, sender],
+            send_sem=a_send.at[g], recv_sem=a_recv.at[g],
             device_id={"wave": other, "lat": lat}, device_id_type=pl.DeviceIdType.MESH,
         )
 
+    def all_rows(g):
+        first = pl.ds(0, N_WAVE - 1)
+        return pltpu.make_async_remote_copy(
+            src_ref=mine[g].at[first], dst_ref=got[g].at[first],
+            send_sem=a_send.at[g], recv_sem=a_recv.at[g],
+            device_id={"wave": peer(1), "lat": lat}, device_id_type=pl.DeviceIdType.MESH,
+        )
+
     def send_rows(g):
-        def one(step, carry):
+        for step in range(1, N_WAVE):
             to_row(g, peer(step), me).start()
-            return carry
-
-        lax.fori_loop(1, N_WAVE, one, 0)
         got[g][me] = mine[g][me]
 
-    def wait_rows(g):
-        def one(step, carry):
-            to_row(g, me, peer(step)).wait_recv()
-            return carry
-
-        lax.fori_loop(1, N_WAVE, one, 0)
-
-    def tables():
-        lons = lons_s[row].astype(jnp.float32)
-        two = 2.0 * lons
-        inverse = 1.0 / jnp.full((8, LANES), two, jnp.float32)
+    lons = lons_s[row].astype(jnp.float32)
+    two = 2.0 * lons
+
+    def reciprocal():
+        return 1.0 / jnp.full((8, LANES), two, jnp.float32)
+
+    def phase_tables():
+        inverse = reciprocal()
 
         def spread(r, carry):
             line = waves_v[pl.ds(r, 1), :].astype(jnp.float32)
@@ -218,7 +235,7 @@
         lax.fori_loop(0, N_WAVE, regroup, 0)
 
         lane = lax.broadcasted_iota(jnp.int32, (8, LANES), 1)
-        first = jnp.where(lane < F, LONS - 1.0, 3.0 * LONS - 1.0).astype(jnp.float32)
+        first = jnp.where(lane < F, BLOCK - 1.0, 3.0 * BLOCK - 1.0).astype(jnp.float32)
 
         def phases(i, carry):
             for j in range(4):
@@ -228,31 +245,37 @@
                 c, s = cos_sin(m * first, two, inverse)
                 c0[rows, :] = weight * c
                 s0[rows, :] = weight * s
-                c, s = cos_sin(m * (4.0 * LONS), two, inverse)
+                c, s = cos_sin(m * (4.0 * BLOCK), two, inverse)
                 c1[rows, :] = c
                 s1[rows, :] = s
             return carry
 
         lax.fori_loop(0, M // 32, phases, 0)
 
+    def block_tables():
+        inverse = reciprocal()
+        line = lax.broadcasted_iota(jnp.int32, (8, LANES), 0).astype(jnp.float32)
         for g, (off, size) in enumerate(GROUPS):
             depth = N_WAVE * size
 
             def columns(i, carry, g=g, off=off, depth=depth):
                 base = pl.multiple_of(N_WAVE * off + i * LANES, LANES)
                 m = jnp.transpose(m_grp[pl.ds(base, LANES), :])[0:8, :]
-                for r in range(0, LONS, 16):
-                    parts = []
-                    for h in range(2):
-                        k = lax.broadcasted_iota(jnp.int32, (8, LANES), 0) + (r + 8 * h)
-                        k = (2 * k - (LONS - 1)).astype(jnp.float32)
-                        parts.append(cos_sin(m * k, two, inverse))
-                    c = jnp.concatenate([p[0] for p in parts], 0)
-                    s = jnp.concatenate([p[1] for p in parts], 0)
-                    at = pl.multiple_of(i * LANES, LANES)
-                    table[g][r : r + 16, pl.ds(at, LANES)] = c.astype(jnp.bfloat16)
-                    at = pl.multiple_of(depth + i * LANES, LANES)
-                    table[g][r : r + 16, pl.ds(at, LANES)] = (-s).astype(jnp.bfloat16)
+                left = pl.ds(pl.multiple_of(i * LANES, LANES), LANES)
+                right = pl.ds(pl.multiple_of(depth + i * LANES, LANES), LANES)
+                fine = [cos_sin(m * (2.0 * line + 16.0 * h), two, inverse) for h in range(2)]
+                fine_c = jnp.concatenate([f[0] for f in fine], 0)
+                fine_s = jnp.concatenate([f[1] for f in fine], 0)
+                for top in range(0, BLOCK // 16, 8):
+                    coarse = m * (32.0 * (line + top) - (BLOCK - 1.0))
+                    coarse_c, coarse_s = cos_sin(coarse, two, inverse)
+                    for j in range(min(8, BLOCK // 16 - top)):
+                        a_c, a_s = coarse_c[j : j + 1], coarse_s[j : j + 1]
+                        c = fine_c * a_c - fine_s * a_s
+                        s = fine_s * a_c + fine_c * a_s
+                        at = 16 * (top + j)
+                        table[g][at : at + 16, left] = c.astype(jnp.bfloat16)
+                        table[g][at : at + 16, right] = (-s).astype(jnp.bfloat16)
                 return carry
 
             lax.fori_loop(0, depth // LANES, columns, 0)
@@ -274,15 +297,12 @@
             a, b = real * c - imag * s, real * s + imag * c
             c, s = c1[rows, :], s1[rows, :]
             at = pl.multiple_of(i * 2 * size, 16)
-            for p in range(2 * QUADS - 1):
+            for p in range(2 * QUADS):
                 columns = slice(LANES * (p % 2), LANES * (p % 2) + LANES)
                 coef[g][p // 2, pl.ds(at, 2 * size), columns] = a.astype(jnp.bfloat16)
                 coef[g][p // 2, pl.ds(depth + at, 2 * size), columns] = b.astype(jnp.bfloat16)
-                if p < 2 * QUADS - 2:
+                if p < 2 * QUADS - 1:
                     a, b = a * c - b * s, a * s + b * c
-            zero = jnp.zeros((2 * size, LANES), jnp.bfloat16)
-            coef[g][QUADS - 1, pl.ds(at, 2 * size), LANES:] = zero
-            coef[g][QUADS - 1, pl.ds(depth + at, 2 * size), LANES:] = zero
             return carry
 
         lax.fori_loop(0, N_WAVE // 2, pair, 0)
@@ -297,48 +317,46 @@
             device_id={"wave": other, "lat": lat}, device_id_type=pl.DeviceIdType.MESH,
         )
 
-    def keep():
-        return pltpu.make_async_copy(out.at[me], raw.at[me], own_sem)
-
     limit = most_lons(row)
     last = len(GROUPS) - 1
 
     copies = [y_copies(g) for g in range(len(GROUPS))]
     legendre_sums(0)
     by_row(0, opp)
-    pl.semaphore_wait(barrier, N_WAVE + 1)
+    pl.semaphore_wait(barrier, 2 + len(plane) + len(line))
     copies[0][0].start()
     copies[0][1].start()
+    tell()
     by_row(0, up)
-    copies[0][2].start()
     by_row(0, dn)
-    copies[0][3].start()
     by_row(0, lat)
     legendre_sums(1)
+    by_row(1, opp)
+    copies[1][0].start()
+    copies[1][1].start()
+    copies[0][2].start()
+    copies[0][3].start()
+    by_row(1, up)
+    by_row(1, dn)
+    by_row(1, lat)
+    phase_tables()
     copies[0][0].wait_recv()
     merge(0, up, 0, from_dn[0])
     copies[0][4].start()
     copies[0][1].wait_recv()
     merge(0, dn, 1, from_up[0])
     copies[0][5].start()
-    by_row(1, opp)
-    copies[1][0].start()
-    copies[1][1].start()
-    by_row(1, up)
-    copies[1][2].start()
-    by_row(1, dn)
-    copies[1][3].start()
-    by_row(1, lat)
-    tables()
+    block_tables()
     copies[1][0].wait_recv()
     merge(1, up, 0, from_dn[1])
-    copies[1][4].start()
     copies[1][1].wait_recv()
     merge(1, dn, 1, from_up[1])
-    copies[1][5].start()
+    hear()
 
     for at in range(2, 6):
         copies[0][at].wait_recv()
+    for at in range(2, 6):
+        copies[1][at].start()
     total(0)
     send_rows(0)
     for at in range(2, 6):
@@ -346,7 +364,7 @@
     total(1)
     send_rows(1)
 
-    wait_rows(0)
+    all_rows(0).wait_recv()
     rotate(0)
 
     def early(quad, carry):
@@ -354,22 +372,24 @@
         return carry
 
     lax.fori_loop(0, QUADS, early, 0)
-    wait_rows(1)
+    all_rows(1).wait_recv()
     rotate(1)
 
     def late(step, carry):
-        quad = lax.rem(me // 4 + step, QUADS)
+        quad = jnp.bitwise_and(me // 8 + step, QUADS - 1)
         value = acc[quad] + product(1, quad)
         lane = lax.broadcasted_iota(jnp.int32, (HALF, LANES), 1)
         for p in range(2):
-            top = value[:HALF, LANES * p : LANES * (p + 1)]
-            bottom = value[HALF:, LANES * p : LANES * (p + 1)]
-            even = jnp.where(lane < F, top, pltpu.roll(bottom, F, 1))
-            odd = jnp.where(lane < F, pltpu.roll(top, F, 1), bottom)
-            out[quad * 4 + 2 * p] = even.astype(jnp.bfloat16)
-            out[quad * 4 + 2 * p + 1] = odd.astype(jnp.bfloat16)
-        for j in range(4):
-            other = quad * 4 + j
+            for c in range(2):
+                columns = slice(LANES * p, LANES * (p + 1))
+                top = value[LONS * c : LONS * c + HALF, columns]
+                bottom = value[LONS * c + HALF : LONS * (c + 1), columns]
+                even = jnp.where(lane < F, top, pltpu.roll(bottom, F, 1))
+                odd = jnp.where(lane < F, pltpu.roll(top, F, 1), bottom)
+                out[quad * 8 + 4 * p + c] = even.astype(jnp.bfloat16)
+                out[quad * 8 + 4 * p + 2 + c] = odd.astype(jnp.bfloat16)
+        for j in range(8):
+            other = quad * 8 + j
 
             @pl.when((other != me) & (other * LONS < limit))
             def _():
@@ -378,37 +398,49 @@
         return carry
 
     lax.fori_loop(0, QUADS, late, 0)
-
-    @pl.when(me * LONS < limit)
-    def _():
-        keep().start()
+    raw[me] = out[me]
+
+    k = me * LONS + lax.broadcasted_iota(jnp.int32, (LONS, F), 0)
 
     def arrived(step, carry):
-        sender = peer(step)
-
-        @pl.when(me * LONS < most_lons(lat * BAND + sender))
+        sender = jnp.bitwise_and(me // 8 - step // 8, 3) * 8 + jnp.bitwise_and(me + step, 7)
+        w = lat * BAND + sender
+        sent = me * LONS < most_lons(w)
+
+        @pl.when(sent & (sender != me))
         def _():
             to_owner(me, sender).wait_recv()
 
+        @pl.when(sent)
+        def _():
+            halves = raw[sender].astype(jnp.float32)
+            lines = jnp.concatenate([halves[:, :F], pltpu.roll(halves, F, 1)[:, :F]], 0)
+            turn[sender] = jnp.where(k < lons_s[w], lines, 0.0).astype(jnp.bfloat16)
+
+        @pl.when(jnp.logical_not(sent))
+        def _():
+            turn[sender] = jnp.zeros((LONS, F), jnp.bfloat16)
+
+        pltpu.make_async_copy(turn.at[sender], grid.at[sender], own_sem).start()
+        return carry
+
+    lax.fori_loop(0, N_WAVE, arrived, 0)
+
+    def gone(step, carry):
         other = peer(step)
 
         @pl.when(other * LONS < limit)
         def _():
             to_owner(other, me).wait_send()
 
-        for g in range(len(GROUPS)):
-            to_row(g, other, me).wait_send()
         return carry
 
-    lax.fori_loop(1, N_WAVE, arrived, 0)
-
-    @pl.when(me * LONS < limit)
-    def _():
-        keep().wait()
-
+    lax.fori_loop(1, N_WAVE, gone, 0)
     for g in range(len(GROUPS)):
+        all_rows(g).wait_send()
         for copy in copies[g]:
             copy.wait_send()
+    pltpu.make_async_copy(turn, grid, own_sem).wait()
 
 
 def local(spectra, legendre, wave_list, cycle_lons):
@@ -425,17 +457,20 @@
     scratch += [pltpu.VMEM((BAND, n, LANES), bf16) for n in sizes]
     scratch += [pltpu.VMEM((N_WAVE, n, LANES), bf16) for n in sizes]
     scratch += [pltpu.VMEM((QUADS, 2 * N_WAVE * n, 2 * LANES), bf16) for n in sizes]
-    scratch += [pltpu.VMEM((LONS, 2 * N_WAVE * n), bf16) for n in sizes]
-    scratch += [pltpu.VMEM((QUADS, LONS, 2 * LANES), f32), pltpu.VMEM((N_WAVE, HALF, LANES), bf16)]
+    scratch += [pltpu.VMEM((BLOCK, 2 * N_WAVE * n), bf16) for n in sizes]
+    scratch += [pltpu.VMEM((QUADS, BLOCK, 2 * LANES), f32)]
+    scratch += [pltpu.VMEM((N_WAVE, HALF, LANES), bf16) for _ in range(2)]
+    scratch += [pltpu.VMEM((BAND, LONS, F), bf16)]
     scratch += [pltpu.VMEM((M, LANES), f32) for _ in range(6)]
     dma = pltpu.SemaphoreType.DMA
     count = len(GROUPS)
-    scratch += [dma((count, 2)), dma((count, 6)), dma((count, 6)), dma((count, N_WAVE))]
-    scratch += [dma((count, N_WAVE)), dma((N_WAVE,)), dma((N_WAVE,)), dma]
-
-    raw = pl.pallas_call(
+    scratch += [dma((count, 2)), dma((count, 6)), dma((count, 6)), dma((count,))]
+    scratch += [dma((count,)), dma((N_WAVE,)), dma((N_WAVE,)), dma]
+    scratch += [pltpu.SemaphoreType.REGULAR]
+
+    return pl.pallas_call(
         kernel,
-        out_shape=jax.ShapeDtypeStruct((BAND, HALF, LANES), bf16),
+        out_shape=jax.ShapeDtypeStruct((BAND, LONS, F), bf16),
         in_specs=[
             pl.BlockSpec(memory_space=pltpu.SMEM),
             pl.BlockSpec(memory_space=pltpu.SMEM),
@@ -450,12 +485,6 @@
         ),
     )(wave_list, cycle_lons, wave_list.reshape(M // LANES, LANES), spectra, legendre)
 
-    first = lax.axis_index("lat") * BAND
-    band_lons = lax.dynamic_slice_in_dim(cycle_lons, first, BAND)
-    k = lax.axis_index("wave") * LONS + jnp.arange(LONS, dtype=jnp.int32)
-    rows = jnp.concatenate([raw[:, :, :F], raw[:, :, F:]], 1)
-    return jnp.where((k[None, :] < band_lons[:, None])[:, :, None], rows, jnp.zeros_like(rows))
-
 
 def solution(mesh):
     in_specs = (P("wave", "lat", None), P("wave", "lat", None), P(), P())

time: 56.2 us -> 50 us (0.89)
  Pallas kernels: 50.9 us -> 47.3 us
  local copies, waits for them, and re-layouts: 3.9 us -> 2.57 us
  other arithmetic: 1.15 us -> 0 us
    pallas_call x1, Pallas kernels: 50.9 us -> 47.3 us  [local(): pl.pallas_call(kernel, out_shape=jax.ShapeDtypeStruct((BAND, LONS, F), bf...]
    pallas_call x0 -> x1, local copies, waits for them, and re-layouts: none -> 2.57 us  [local(): pl.pallas_call(kernel, out_shape=jax.ShapeDtypeStruct((BAND, LONS, F), bf...]
    slice x1 -> x0, local copies, waits for them, and re-layouts: 1.61 us -> none  [local(): rows = jnp.concatenate([raw[:, :, :F], raw[:, :, F:]], 1)]
    select_n x1 -> x0, local copies, waits for them, and re-layouts: 1.57 us -> none  [local(): jnp.where((k[None, :] < band_lons[:, None])[:, :, None], rows, jnp.zeros_...]
    select_n x1 -> x0, other arithmetic: 1.07 us -> none  [local(): jnp.where((k[None, :] < band_lons[:, None])[:, :, None], rows, jnp.zeros_...]
    dynamic_slice x1 -> x0, local copies, waits for them, and re-layouts: 0.73 us -> none  [local(): band_lons = lax.dynamic_slice_in_dim(cycle_lons, first, BAND)]
where the time goes in v2:
time: 50 us; the launch traced here: 49.8 us
  Pallas kernels  47.3 us (95%)
  local copies, waits for them, and re-layouts  2.57 us (5%)
    pallas_call x1, Pallas kernels, local(): pl.pallas_call(kernel, out_shape=jax.ShapeDtypeStruct((BAND, LONS, F), bf...  47.3 us
    pallas_call x1, local copies, waits for them, and re-layouts, local(): pl.pallas_call(kernel, out_shape=jax.ShapeDtypeStruct((BAND, LONS, F), bf...  2.57 us

profile of v2, /device:TPU:1, one launch (start us, length us, event | category | flops | bytes accessed | tf_op | source)
XLA Modules:
  0.0 49.8 jit_solution(14889063070394600046)
XLA Ops:
  0.0 47.3 %shard_map.46 = bf16[32,176,64]{2,1,0:T(8,128)(2,1)} custom-call(s32[1280]{0:T(1024)} %waves_s.1, s32[128]{0:T(128)} %lons_s.1, s32[10,128]{1,0:T(8,128)} %bitcast.1, bf16[40,320,128]{2,1,0:T(8,128)(2,1)} %spectra.1, bf16[40,320,128]{2,1,0:T(8,128)(2,1)} %legendre.1), custom_call_target="tpu_custom_call" | custom-call | tf_op jit(solution)/shard_map/pallas_call | solution.py:471
  47.3 2.6 %copy.5 = bf16[32,176,64]{1,2,0:T(8,128)(2,1)} copy(bf16[32,176,64]{2,1,0:T(8,128)(2,1)} %shard_map.46) | data formatting | bytes 1441792 | tf_op jit(solution)/shard_map/pallas_call | solution.py:471

commit v3 on v2

--- a/solution.py
+++ b/solution.py
@@ -23,6 +23,7 @@
 BLOCK = 2 * LONS
 QUADS = N_WAVE // 8
 GROUPS = ((0, 24), (24, 16))
+CHUNK = 8
 
 COS_TERMS = (
     0.999999009718151, -19.738932854525416, 64.92691787698224,
@@ -47,13 +48,13 @@
     return c, s * u
 
 
-def kernel(waves_s, lons_s, waves_v, spectra, legendre, grid, *scratch):
+def kernel(waves_s, lons_s, waves_v, spectra, legendre, raw, *scratch):
     names = iter(scratch)
     spec, leg, partial = next(names), next(names), next(names)
     bands, from_dn, from_up, sum_dn, sum_up, mine, got, coef, table = (
         [next(names) for _ in GROUPS] for _ in range(9)
     )
-    acc, out, raw, turn, m_nat, m_grp, c0, s0, c1, s1 = (next(names) for _ in range(10))
+    acc, out, m_nat, m_grp, c0, s0, c1, s1 = (next(names) for _ in range(8))
     in_sem, y_send, y_recv, a_send, a_recv, o_send, o_recv, own_sem, line_sem = names
 
     me = lax.axis_index("wave")
@@ -71,16 +72,14 @@
     def peer(step):
         return jnp.bitwise_and(me + step, N_WAVE - 1)
 
-    def load(g, which):
-        off, size = GROUPS[g]
+    def load(chunk, which):
         source, target = ((spectra, spec), (legendre, leg))[which]
-        return pltpu.make_async_copy(
-            source.at[pl.ds(off, size)], target.at[pl.ds(off, size)], in_sem.at[g, which]
-        )
-
-    for g in range(len(GROUPS)):
+        slots = pl.ds(chunk * CHUNK, CHUNK)
+        return pltpu.make_async_copy(source.at[slots], target.at[slots], in_sem.at[chunk, which])
+
+    for chunk in range(SLOTS // CHUNK):
         for which in range(2):
-            load(g, which).start()
+            load(chunk, which).start()
 
     barrier = pltpu.get_barrier_semaphore()
     for other in (up, dn):
@@ -132,8 +131,6 @@
 
     def legendre_sums(g):
         off, size = GROUPS[g]
-        load(g, 0).wait()
-        load(g, 1).wait()
 
         def slot(s, carry):
             live = M - waves_s[me * SLOTS + off + s] - lat * DEPTH
@@ -145,7 +142,12 @@
             )
             return carry
 
-        lax.fori_loop(0, size, slot, 0, unroll=4)
+        def several(i, carry):
+            for which in range(2):
+                load(off // CHUNK + i, which).wait()
+            return lax.fori_loop(0, CHUNK, lambda j, c: slot(i * CHUNK + j, c), carry, unroll=4)
+
+        lax.fori_loop(0, size // CHUNK, several, 0)
 
     def by_row(g, band):
         size = GROUPS[g][1]
@@ -316,6 +318,9 @@
             send_sem=o_send.at[other], recv_sem=o_recv.at[sender],
             device_id={"wave": other, "lat": lat}, device_id_type=pl.DeviceIdType.MESH,
         )
+
+    def far_first(step):
+        return jnp.where(step == 0, 2, jnp.where(step == 1, 1, jnp.where(step == 2, 3, 0)))
 
     limit = most_lons(row)
     last = len(GROUPS) - 1
@@ -376,7 +381,7 @@
     rotate(1)
 
     def late(step, carry):
-        quad = jnp.bitwise_and(me // 8 + step, QUADS - 1)
+        quad = jnp.bitwise_and(me // 8 + far_first(step), QUADS - 1)
         value = acc[quad] + product(1, quad)
         lane = lax.broadcasted_iota(jnp.int32, (HALF, LANES), 1)
         for p in range(2):
@@ -398,30 +403,16 @@
         return carry
 
     lax.fori_loop(0, QUADS, late, 0)
-    raw[me] = out[me]
-
-    k = me * LONS + lax.broadcasted_iota(jnp.int32, (LONS, F), 0)
+    keep = pltpu.make_async_copy(out.at[me], raw.at[me], own_sem)
+    keep.start()
 
     def arrived(step, carry):
-        sender = jnp.bitwise_and(me // 8 - step // 8, 3) * 8 + jnp.bitwise_and(me + step, 7)
-        w = lat * BAND + sender
-        sent = me * LONS < most_lons(w)
-
-        @pl.when(sent & (sender != me))
+        sender = jnp.bitwise_and(me // 8 - far_first(step // 8), 3) * 8 + jnp.bitwise_and(me + step, 7)
+
+        @pl.when((me * LONS < most_lons(lat * BAND + sender)) & (sender != me))
         def _():
             to_owner(me, sender).wait_recv()
 
-        @pl.when(sent)
-        def _():
-            halves = raw[sender].astype(jnp.float32)
-            lines = jnp.concatenate([halves[:, :F], pltpu.roll(halves, F, 1)[:, :F]], 0)
-            turn[sender] = jnp.where(k < lons_s[w], lines, 0.0).astype(jnp.bfloat16)
-
-        @pl.when(jnp.logical_not(sent))
-        def _():
-            turn[sender] = jnp.zeros((LONS, F), jnp.bfloat16)
-
-        pltpu.make_async_copy(turn.at[sender], grid.at[sender], own_sem).start()
         return carry
 
     lax.fori_loop(0, N_WAVE, arrived, 0)
@@ -440,7 +431,16 @@
         all_rows(g).wait_send()
         for copy in copies[g]:
             copy.wait_send()
-    pltpu.make_async_copy(turn, grid, own_sem).wait()
+    keep.wait()
+
+
+def unpack_kernel(lons_s, raw, grid):
+    first = lax.axis_index("lat") * BAND
+    k = lax.axis_index("wave") * LONS + lax.broadcasted_iota(jnp.int32, (F, LONS), 1)
+    for w in range(BAND):
+        turned = jnp.transpose(raw[w]).astype(jnp.float32)
+        line = jnp.concatenate([turned[:F], turned[F:]], 1)
+        grid[w] = jnp.where(k < lons_s[first + w], line, 0.0).astype(jnp.bfloat16)
 
 
 def local(spectra, legendre, wave_list, cycle_lons):
@@ -459,18 +459,17 @@
     scratch += [pltpu.VMEM((QUADS, 2 * N_WAVE * n, 2 * LANES), bf16) for n in sizes]
     scratch += [pltpu.VMEM((BLOCK, 2 * N_WAVE * n), bf16) for n in sizes]
     scratch += [pltpu.VMEM((QUADS, BLOCK, 2 * LANES), f32)]
-    scratch += [pltpu.VMEM((N_WAVE, HALF, LANES), bf16) for _ in range(2)]
-    scratch += [pltpu.VMEM((BAND, LONS, F), bf16)]
+    scratch += [pltpu.VMEM((N_WAVE, HALF, LANES), bf16)]
     scratch += [pltpu.VMEM((M, LANES), f32) for _ in range(6)]
     dma = pltpu.SemaphoreType.DMA
     count = len(GROUPS)
-    scratch += [dma((count, 2)), dma((count, 6)), dma((count, 6)), dma((count,))]
+    scratch += [dma((SLOTS // CHUNK, 2)), dma((count, 6)), dma((count, 6)), dma((count,))]
     scratch += [dma((count,)), dma((N_WAVE,)), dma((N_WAVE,)), dma]
     scratch += [pltpu.SemaphoreType.REGULAR]
 
-    return pl.pallas_call(
+    raw = pl.pallas_call(
         kernel,
-        out_shape=jax.ShapeDtypeStruct((BAND, LONS, F), bf16),
+        out_shape=jax.ShapeDtypeStruct((BAND, HALF, LANES), bf16),
         in_specs=[
             pl.BlockSpec(memory_space=pltpu.SMEM),
             pl.BlockSpec(memory_space=pltpu.SMEM),
@@ -484,6 +483,13 @@
             collective_id=0, has_side_effects=True, vmem_limit_bytes=56 * 2**20
         ),
     )(wave_list, cycle_lons, wave_list.reshape(M // LANES, LANES), spectra, legendre)
+    grid = pl.pallas_call(
+        unpack_kernel,
+        out_shape=jax.ShapeDtypeStruct((BAND, F, LONS), bf16),
+        in_specs=[pl.BlockSpec(memory_space=pltpu.SMEM), pl.BlockSpec(memory_space=pltpu.VMEM)],
+        out_specs=pl.BlockSpec(memory_space=pltpu.VMEM),
+    )(cycle_lons, raw)
+    return jnp.transpose(grid, (0, 2, 1))
 
 
 def solution(mesh):

time: 50 us -> 45.6 us (0.912)
  local copies, waits for them, and re-layouts: 2.57 us -> 0 us
  Pallas kernels: 47.3 us -> 45.4 us
    pallas_call x1 -> x0, local copies, waits for them, and re-layouts: 2.57 us -> none  [local(): pl.pallas_call(kernel, out_shape=jax.ShapeDtypeStruct((BAND, LONS, F), bf...]
    pallas_call x1 -> x2, Pallas kernels: 47.3 us -> 45.4 us  [the longest x1 42.8 us: local(): pl.pallas_call(kernel, out_shape=jax.ShapeDtypeStruct((BAND, HALF, LANES)...]
where the time goes in v3:
time: 45.6 us; the launch traced here: 45.5 us
  Pallas kernels  45.4 us (100%)
    pallas_call x1, Pallas kernels, local(): pl.pallas_call(kernel, out_shape=jax.ShapeDtypeStruct((BAND, HALF, LANES)...  42.8 us
    pallas_call x1, Pallas kernels, local(): pl.pallas_call(unpack_kernel, out_shape=jax.ShapeDtypeStruct((BAND, F, LO...  2.66 us

profile of v3, /device:TPU:1, one launch (start us, length us, event | category | flops | bytes accessed | tf_op | source)
XLA Modules:
  0.0 45.5 jit_solution(7758730706325541841)
XLA Ops:
  0.0 42.8 %shard_map.46.raw = bf16[32,88,128]{2,1,0:T(8,128)(2,1)} custom-call(s32[1280]{0:T(1024)} %waves_s.1, s32[128]{0:T(128)} %lons_s.3, s32[10,128]{1,0:T(8,128)} %bitcast.2, bf16[40,320,128]{2,1,0:T(8,128)(2,1)} %spectra.1, bf16[40,320,128]{2,1,0:T(8,128)(2,1)} %legendre.1), custom_call_target="tpu_custom_call" | custom-call | tf_op jit(solution)/shard_map/pallas_call | solution.py:470
  42.8 2.7 %shard_map.47 = bf16[32,64,176]{2,1,0:T(8,128)(2,1)} custom-call(s32[128]{0:T(128)} %lons_s.3, bf16[32,88,128]{2,1,0:T(8,128)(2,1)} %shard_map.46.raw), custom_call_target="tpu_custom_call" | custom-call | tf_op jit(solution)/shard_map/pallas_call | solution.py:486

commit v4 on v3

--- a/solution.py
+++ b/solution.py
@@ -22,8 +22,12 @@
 LANES = 128
 BLOCK = 2 * LONS
 QUADS = N_WAVE // 8
-GROUPS = ((0, 24), (24, 16))
+GROUPS = ((0, 16), (16, 24))
 CHUNK = 8
+FAR_FIRST = sorted(
+    [(x, z, c) for x in range(4) for z in range(4) for c in range(2) if x or z or c],
+    key=lambda s: (-min(s[0], 4 - s[0]) - min(s[1], 4 - s[1]), s),
+)
 
 COS_TERMS = (
     0.999999009718151, -19.738932854525416, 64.92691787698224,
@@ -145,7 +149,7 @@
         def several(i, carry):
             for which in range(2):
                 load(off // CHUNK + i, which).wait()
-            return lax.fori_loop(0, CHUNK, lambda j, c: slot(i * CHUNK + j, c), carry, unroll=4)
+            return lax.fori_loop(0, CHUNK, lambda j, c: slot(i * CHUNK + j, c), carry, unroll=8)
 
         lax.fori_loop(0, size // CHUNK, several, 0)
 
@@ -160,7 +164,7 @@
             )
             return carry
 
-        lax.fori_loop(0, BAND // 2, pair, 0, unroll=4)
+        lax.fori_loop(0, BAND // 2, pair, 0, unroll=16)
 
     def merge(g, band, at, received):
         half = BAND // 2 * GROUPS[g][1]
@@ -173,7 +177,7 @@
             bands[g][band, rows, :] = total.astype(jnp.bfloat16)
             return carry
 
-        lax.fori_loop(0, 4, part, 0)
+        lax.fori_loop(0, 4, part, 0, unroll=4)
 
     def total(g):
         size = GROUPS[g][1]
@@ -187,7 +191,7 @@
             mine[g][2 * i + 1] = value[size:].astype(jnp.bfloat16)
             return carry
 
-        lax.fori_loop(0, BAND // 2, pair, 0, unroll=2)
+        lax.fori_loop(0, BAND // 2, pair, 0, unroll=8)
 
     def to_row(g, other, sender):
         return pltpu.make_async_remote_copy(
@@ -205,8 +209,8 @@
         )
 
     def send_rows(g):
-        for step in range(1, N_WAVE):
-            to_row(g, peer(step), me).start()
+        for shift in FAR_FIRST:
+            to_row(g, shifted(*shift), me).start()
         got[g][me] = mine[g][me]
 
     lons = lons_s[row].astype(jnp.float32)
@@ -225,7 +229,7 @@
             )
             return carry
 
-        lax.fori_loop(0, M // LANES, spread, 0)
+        lax.fori_loop(0, M // LANES, spread, 0, unroll=5)
 
         def regroup(v, carry):
             for off, size in GROUPS:
@@ -234,7 +238,7 @@
                 ]
             return carry
 
-        lax.fori_loop(0, N_WAVE, regroup, 0)
+        lax.fori_loop(0, N_WAVE, regroup, 0, unroll=4)
 
         lane = lax.broadcasted_iota(jnp.int32, (8, LANES), 1)
         first = jnp.where(lane < F, BLOCK - 1.0, 3.0 * BLOCK - 1.0).astype(jnp.float32)
@@ -252,7 +256,7 @@
                 s1[rows, :] = s
             return carry
 
-        lax.fori_loop(0, M // 32, phases, 0)
+        lax.fori_loop(0, M // 32, phases, 0, unroll=2)
 
     def block_tables():
         inverse = reciprocal()
@@ -307,7 +311,7 @@
                     a, b = a * c - b * s, a * s + b * c
             return carry
 
-        lax.fori_loop(0, N_WAVE // 2, pair, 0)
+        lax.fori_loop(0, N_WAVE // 2, pair, 0, unroll=4)
 
     def product(g, quad):
         return jnp.dot(table[g][...], coef[g][quad], preferred_element_type=jnp.float32)
@@ -320,7 +324,7 @@
         )
 
     def far_first(step):
-        return jnp.where(step == 0, 2, jnp.where(step == 1, 1, jnp.where(step == 2, 3, 0)))
+        return jnp.where(step == 0, 2, jnp.where(step == 1, 3, jnp.where(step == 2, 1, 0)))
 
     limit = most_lons(row)
     last = len(GROUPS) - 1
@@ -356,12 +360,12 @@
     merge(1, up, 0, from_dn[1])
     copies[1][1].wait_recv()
     merge(1, dn, 1, from_up[1])
+    for at in range(2, 6):
+        copies[1][at].start()
     hear()
 
     for at in range(2, 6):
         copies[0][at].wait_recv()
-    for at in range(2, 6):
-        copies[1][at].start()
     total(0)
     send_rows(0)
     for at in range(2, 6):
@@ -406,17 +410,6 @@
     keep = pltpu.make_async_copy(out.at[me], raw.at[me], own_sem)
     keep.start()
 
-    def arrived(step, carry):
-        sender = jnp.bitwise_and(me // 8 - far_first(step // 8), 3) * 8 + jnp.bitwise_and(me + step, 7)
-
-        @pl.when((me * LONS < most_lons(lat * BAND + sender)) & (sender != me))
-        def _():
-            to_owner(me, sender).wait_recv()
-
-        return carry
-
-    lax.fori_loop(0, N_WAVE, arrived, 0)
-
     def gone(step, carry):
         other = peer(step)
 
@@ -431,6 +424,16 @@
         all_rows(g).wait_send()
         for copy in copies[g]:
             copy.wait_send()
+    def arrived(step, carry):
+        sender = jnp.bitwise_and(me // 8 - far_first(step // 8), 3) * 8 + jnp.bitwise_and(me + step, 7)
+
+        @pl.when((me * LONS < most_lons(lat * BAND + sender)) & (sender != me))
+        def _():
+            to_owner(me, sender).wait_recv()
+
+        return carry
+
+    lax.fori_loop(0, N_WAVE, arrived, 0)
     keep.wait()
 
 

time: 45.6 us -> 43.1 us (0.945)
  Pallas kernels: 45.4 us -> 43 us
    pallas_call x1, Pallas kernels: 42.8 us -> 40.3 us  [local(): pl.pallas_call(kernel, out_shape=jax.ShapeDtypeStruct((BAND, HALF, LANES)...]
where the time goes in v4:
time: 43.1 us; the launch traced here: 43 us
  Pallas kernels  43 us (100%)
    pallas_call x1, Pallas kernels, local(): pl.pallas_call(kernel, out_shape=jax.ShapeDtypeStruct((BAND, HALF, LANES)...  40.3 us
    pallas_call x1, Pallas kernels, local(): pl.pallas_call(unpack_kernel, out_shape=jax.ShapeDtypeStruct((BAND, F, LO...  2.66 us

profile of v4, /device:TPU:1, one launch (start us, length us, event | category | flops | bytes accessed | tf_op | source)
XLA Modules:
  0.0 43.0 jit_solution(13422331683524088040)
XLA Ops:
  0.0 40.3 %shard_map.46.raw = bf16[32,88,128]{2,1,0:T(8,128)(2,1)} custom-call(s32[1280]{0:T(1024)} %waves_s.1, s32[128]{0:T(128)} %lons_s.3, s32[10,128]{1,0:T(8,128)} %bitcast.2, bf16[40,320,128]{2,1,0:T(8,128)(2,1)} %spectra.1, bf16[40,320,128]{2,1,0:T(8,128)(2,1)} %legendre.1), custom_call_target="tpu_custom_call" | custom-call | tf_op jit(solution)/shard_map/pallas_call | solution.py:473
  40.3 2.7 %shard_map.47 = bf16[32,64,176]{2,1,0:T(8,128)(2,1)} custom-call(s32[128]{0:T(128)} %lons_s.3, bf16[32,88,128]{2,1,0:T(8,128)(2,1)} %shard_map.46.raw), custom_call_target="tpu_custom_call" | custom-call | tf_op jit(solution)/shard_map/pallas_call | solution.py:489

commit v5 on v4

--- a/solution.py
+++ b/solution.py
@@ -54,9 +54,9 @@
 
 def kernel(waves_s, lons_s, waves_v, spectra, legendre, raw, *scratch):
     names = iter(scratch)
-    spec, leg, partial = next(names), next(names), next(names)
-    bands, from_dn, from_up, sum_dn, sum_up, mine, got, coef, table = (
-        [next(names) for _ in GROUPS] for _ in range(9)
+    spec, leg = next(names), next(names)
+    partial, bands, from_dn, from_up, sum_dn, sum_up, mine, got, coef, table = (
+        [next(names) for _ in GROUPS] for _ in range(10)
     )
     acc, out, m_nat, m_grp, c0, s0, c1, s1 = (next(names) for _ in range(8))
     in_sem, y_send, y_recv, a_send, a_recv, o_send, o_recv, own_sem, line_sem = names
@@ -140,7 +140,7 @@
             live = M - waves_s[me * SLOTS + off + s] - lat * DEPTH
             offsets = lax.broadcasted_iota(jnp.int32, (DEPTH, LANES), 0)
             masked = jnp.where(offsets < live, spec[off + s].astype(jnp.float32), 0.0)
-            partial[pl.ds(pl.multiple_of(s * NLW, NLW), NLW), :] = lax.dot_general(
+            partial[g][pl.ds(pl.multiple_of(s * NLW, NLW), NLW), :] = lax.dot_general(
                 leg[off + s], masked.astype(jnp.bfloat16), (((0,), (0,)), ((), ())),
                 preferred_element_type=jnp.float32,
             )
@@ -158,7 +158,7 @@
 
         def pair(i, carry):
             first = band * BAND + 2 * i
-            rows = [partial[pl.ds(first + j, size, stride=NLW), :] for j in range(2)]
+            rows = [partial[g][pl.ds(first + j, size, stride=NLW), :] for j in range(2)]
             bands[g][band, pl.ds(pl.multiple_of(i * 2 * size, 2 * size), 2 * size), :] = (
                 jnp.concatenate(rows, 0).astype(jnp.bfloat16)
             )
@@ -337,31 +337,33 @@
     copies[0][1].start()
     tell()
     by_row(0, up)
+    copies[0][2].start()
     by_row(0, dn)
-    by_row(0, lat)
+    copies[0][3].start()
     legendre_sums(1)
     by_row(1, opp)
     copies[1][0].start()
     copies[1][1].start()
-    copies[0][2].start()
-    copies[0][3].start()
-    by_row(1, up)
-    by_row(1, dn)
-    by_row(1, lat)
-    phase_tables()
     copies[0][0].wait_recv()
     merge(0, up, 0, from_dn[0])
     copies[0][4].start()
     copies[0][1].wait_recv()
     merge(0, dn, 1, from_up[0])
     copies[0][5].start()
-    block_tables()
+    by_row(1, up)
+    copies[1][2].start()
+    by_row(1, dn)
+    copies[1][3].start()
+    phase_tables()
     copies[1][0].wait_recv()
     merge(1, up, 0, from_dn[1])
+    copies[1][4].start()
     copies[1][1].wait_recv()
     merge(1, dn, 1, from_up[1])
-    for at in range(2, 6):
-        copies[1][at].start()
+    copies[1][5].start()
+    by_row(0, lat)
+    by_row(1, lat)
+    block_tables()
     hear()
 
     for at in range(2, 6):
@@ -452,8 +454,8 @@
     scratch = [
         pltpu.VMEM((SLOTS, DEPTH, LANES), bf16),
         pltpu.VMEM((SLOTS, DEPTH, LANES), bf16),
-        pltpu.VMEM((max(sizes) * NLW, LANES), f32),
     ]
+    scratch += [pltpu.VMEM((n * NLW, LANES), f32) for n in sizes]
     scratch += [pltpu.VMEM((N_LAT, BAND * n, LANES), bf16) for n in sizes]
     for rows in (BAND // 2, BAND // 2, BAND, BAND):
         scratch += [pltpu.VMEM((rows * n, LANES), bf16) for n in sizes]

time: 43.1 us -> 42.6 us (0.988)
  Pallas kernels: 43 us -> 42.4 us
    pallas_call x1, Pallas kernels: 40.3 us -> 39.8 us  [local(): pl.pallas_call(kernel, out_shape=jax.ShapeDtypeStruct((BAND, HALF, LANES)...]
where the time goes in v5:
time: 42.6 us; the launch traced here: 42.4 us
  Pallas kernels  42.4 us (100%)
    pallas_call x1, Pallas kernels, local(): pl.pallas_call(kernel, out_shape=jax.ShapeDtypeStruct((BAND, HALF, LANES)...  39.8 us
    pallas_call x1, Pallas kernels, local(): pl.pallas_call(unpack_kernel, out_shape=jax.ShapeDtypeStruct((BAND, F, LO...  2.66 us

profile of v5, /device:TPU:1, one launch (start us, length us, event | category | flops | bytes accessed | tf_op | source)
XLA Modules:
  0.0 42.4 jit_solution(12184002436768633961)
XLA Ops:
  0.0 39.8 %shard_map.46.raw = bf16[32,88,128]{2,1,0:T(8,128)(2,1)} custom-call(s32[1280]{0:T(1024)} %waves_s.1, s32[128]{0:T(128)} %lons_s.3, s32[10,128]{1,0:T(8,128)} %bitcast.2, bf16[40,320,128]{2,1,0:T(8,128)(2,1)} %spectra.1, bf16[40,320,128]{2,1,0:T(8,128)(2,1)} %legendre.1), custom_call_target="tpu_custom_call" | custom-call | tf_op jit(solution)/shard_map/pallas_call | solution.py:475
  39.8 2.7 %shard_map.47 = bf16[32,64,176]{2,1,0:T(8,128)(2,1)} custom-call(s32[128]{0:T(128)} %lons_s.3, bf16[32,88,128]{2,1,0:T(8,128)(2,1)} %shard_map.46.raw), custom_call_target="tpu_custom_call" | custom-call | tf_op jit(solution)/shard_map/pallas_call | solution.py:491

commit v6 on v5

--- a/solution.py
+++ b/solution.py
@@ -379,15 +379,17 @@
     rotate(0)
 
     def early(quad, carry):
-        acc[quad] = product(0, quad)
+        @pl.when(quad * 8 * LONS < limit)
+        def _():
+            acc[quad] = product(0, quad)
+
         return carry
 
     lax.fori_loop(0, QUADS, early, 0)
     all_rows(1).wait_recv()
     rotate(1)
 
-    def late(step, carry):
-        quad = jnp.bitwise_and(me // 8 + far_first(step), QUADS - 1)
+    def finish(quad):
         value = acc[quad] + product(1, quad)
         lane = lax.broadcasted_iota(jnp.int32, (HALF, LANES), 1)
         for p in range(2):
@@ -406,11 +408,22 @@
             def _():
                 to_owner(other, me).start()
 
+    def late(step, carry):
+        quad = jnp.bitwise_and(me // 8 + far_first(step), QUADS - 1)
+
+        @pl.when(quad * 8 * LONS < limit)
+        def _():
+            finish(quad)
+
         return carry
 
     lax.fori_loop(0, QUADS, late, 0)
     keep = pltpu.make_async_copy(out.at[me], raw.at[me], own_sem)
-    keep.start()
+
+    @pl.when(me * LONS < limit)
+    def _():
+        keep.start()
+
 
     def gone(step, carry):
         other = peer(step)
@@ -436,7 +449,10 @@
         return carry
 
     lax.fori_loop(0, N_WAVE, arrived, 0)
-    keep.wait()
+
+    @pl.when(me * LONS < limit)
+    def _():
+        keep.wait()
 
 
 def unpack_kernel(lons_s, raw, grid):

time: 42.6 us -> 41.9 us (0.984)
  Pallas kernels: 42.4 us -> 41.8 us
    pallas_call x1, Pallas kernels: 39.8 us -> 39.1 us  [local(): pl.pallas_call(kernel, out_shape=jax.ShapeDtypeStruct((BAND, HALF, LANES)...]
where the time goes in v6:
time: 41.9 us; the launch traced here: 41.8 us
  Pallas kernels  41.8 us (100%)
    pallas_call x1, Pallas kernels, local(): pl.pallas_call(kernel, out_shape=jax.ShapeDtypeStruct((BAND, HALF, LANES)...  39.1 us
    pallas_call x1, Pallas kernels, local(): pl.pallas_call(unpack_kernel, out_shape=jax.ShapeDtypeStruct((BAND, F, LO...  2.66 us

profile of v6, /device:TPU:1, one launch (start us, length us, event | category | flops | bytes accessed | tf_op | source)
XLA Modules:
  0.0 41.8 jit_solution(11140981117118043098)
XLA Ops:
  0.0 39.1 %shard_map.46.raw = bf16[32,88,128]{2,1,0:T(8,128)(2,1)} custom-call(s32[1280]{0:T(1024)} %waves_s.1, s32[128]{0:T(128)} %lons_s.3, s32[10,128]{1,0:T(8,128)} %bitcast.2, bf16[40,320,128]{2,1,0:T(8,128)(2,1)} %spectra.1, bf16[40,320,128]{2,1,0:T(8,128)(2,1)} %legendre.1), custom_call_target="tpu_custom_call" | custom-call | tf_op jit(solution)/shard_map/pallas_call | solution.py:491
  39.1 2.7 %shard_map.47 = bf16[32,64,176]{2,1,0:T(8,128)(2,1)} custom-call(s32[128]{0:T(128)} %lons_s.3, bf16[32,88,128]{2,1,0:T(8,128)(2,1)} %shard_map.46.raw), custom_call_target="tpu_custom_call" | custom-call | tf_op jit(solution)/shard_map/pallas_call | solution.py:507
